TPU v7x, 128 devices: a whole 4x4x4 slice. The times are simulated.
128 devices in a mesh: dp: 4 (over z), expert: 32 (over y, x, core).
Axes of the slice: x: 4, y: 4, z: 4, core: 2. Of those that a mesh axis runs over, the one named last changes fastest.
Arguments:
- tokens: bfloat16 [16384, 4096], P(('dp', 'expert')), may hold values from -6 to 6
- expert_ids: int32 [16384, 2], P(('dp', 'expert')), may hold values from 0 to 31, all different within a row; in each aligned block of 128 rows (0 to 127, 128 to 255, ...) at most 9 rows name the same one
- router_probs: float32 [16384, 2], P(('dp', 'expert')), may hold values from 0.1 to 1
- w_gate: bfloat16 [32, 1024, 4096], P('expert', 'dp'), may hold values from -0.09375 to 0.09375
- w_up: bfloat16 [32, 1024, 4096], P('expert', 'dp'), may hold values from -0.09375 to 0.09375
- w_down: bfloat16 [32, 1024, 4096], P('expert', 'dp'), may hold values from -0.1875 to 0.1875
- out_grad: bfloat16 [16384, 4096], P(('dp', 'expert')), may hold values from -6 to 6
Outputs:
- mixed: bfloat16 [16384, 4096], P(('dp', 'expert'))
- input_grad: bfloat16 [16384, 4096], P(('dp', 'expert'))
- prob_grad: float32 [16384, 2], P(('dp', 'expert'))
- grad_gate: bfloat16 [32, 1024, 4096], P('expert', 'dp')
- grad_up: bfloat16 [32, 1024, 4096], P('expert', 'dp')
- grad_down: bfloat16 [32, 1024, 4096], P('expert', 'dp')
Inputs may be any that keep to these rules, and one draw needn't show every extreme that they name: `expert_ids`: each row names 2 different experts. Among the rows of one device no expert is named more than 9 times, a bound that some block reaches.
All inputs are finite; a program needn't handle non-finite values.
Results may differ from a plain program's by a relative error of at most 0.018.
Values may be sent and summed in bfloat16 or wider, within the bound.
No kernel may reach another device: no remote copies, remote signals or barrier semaphores. Data moves between devices by JAX's collectives and lax.ppermute only.
A program may use at most 192 MiB of HBM per device.

v0:
```python
import jax
import jax.numpy as jnp
from jax import lax
from jax.sharding import PartitionSpec as P


def deliver(stacked):
    moved_rows = lax.all_to_all(stacked, "expert", split_axis=1, concat_axis=1, tiled=True)
    arrived = lax.all_gather(moved_rows[None], "dp", axis=0, tiled=True)
    return arrived


def send_back(stacked):
    return lax.all_to_all(stacked, "expert", split_axis=1, concat_axis=1, tiled=True)


def on_device(tokens, expert_ids, router_probs, w_gate, w_up, w_down, out_grad):
    tok_rows, model_width = tokens.shape
    top_count = expert_ids.shape[1]
    local_experts = w_gate.shape[0]
    n_expert = lax.axis_size("expert")
    n_replica = lax.axis_size("dp")
    experts = local_experts * n_expert
    slot_depth = max(2, tok_rows * top_count * 9 // (8 * experts))
    slot_total = experts * slot_depth
    blocks = n_replica * n_expert
    flat_ids = expert_ids.reshape(-1)
    onehot = (flat_ids[:, None] == jnp.arange(experts, dtype=jnp.int32)[None, :]).astype(jnp.int32)
    earlier = jnp.cumsum(onehot, axis=0) - onehot
    rank_of = jnp.sum(earlier * onehot, axis=1)
    slot_of = flat_ids * slot_depth + rank_of
    selector = (jnp.arange(slot_total, dtype=jnp.int32)[:, None] == slot_of[None, :]).astype(
        jnp.bfloat16
    )
    by_token = jnp.sum(selector.reshape(slot_total, tok_rows, top_count), axis=2)
    send_tokens = jnp.dot(by_token, tokens, preferred_element_type=jnp.float32).astype(jnp.bfloat16)
    send_tokens = send_tokens.reshape(n_expert, local_experts, slot_depth, model_width)
    scaled = (
        router_probs.reshape(-1)[:, None]
        * jnp.repeat(out_grad, top_count, axis=0).astype(jnp.float32)
    ).astype(jnp.bfloat16)
    send_grads = jnp.dot(selector, scaled, preferred_element_type=jnp.float32).astype(jnp.bfloat16)
    send_grads = send_grads.reshape(n_expert, local_experts, slot_depth, model_width)
    block_shape = (blocks, local_experts, slot_depth, model_width)
    rows_in = deliver(send_tokens[None])[:, 0].reshape(block_shape)
    gate_proj = jnp.einsum("sxmd,xfd->sxmf", rows_in, w_gate, preferred_element_type=jnp.float32)
    up_proj = jnp.einsum("sxmd,xfd->sxmf", rows_in, w_up, preferred_element_type=jnp.float32)
    sigmoid_gate = jax.nn.sigmoid(gate_proj)
    activated = gate_proj * sigmoid_gate
    hidden = (activated * up_proj).astype(jnp.bfloat16)
    expert_out = lax.psum_scatter(
        jnp.einsum("sxmf,xfd->sxmd", hidden, w_down, preferred_element_type=jnp.float32).astype(
            jnp.bfloat16
        ),
        "dp",
        scatter_dimension=0,
        tiled=True,
    )
    back_out = send_back(expert_out[None])[0]
    grads_in = deliver(send_grads[None])[:, 0].reshape(block_shape)
    d_hidden = jnp.einsum("sxmd,xfd->sxmf", grads_in, w_down, preferred_element_type=jnp.float32)
    grad_down = jnp.einsum(
        "sxmf,sxmd->xfd", hidden, grads_in, preferred_element_type=jnp.float32
    ).astype(jnp.bfloat16)
    d_gate = (d_hidden * up_proj * sigmoid_gate * (1.0 + gate_proj * (1.0 - sigmoid_gate))).astype(
        jnp.bfloat16
    )
    d_up = (d_hidden * activated).astype(jnp.bfloat16)
    grad_gate = jnp.einsum(
        "sxmf,sxmd->xfd", d_gate, rows_in, preferred_element_type=jnp.float32
    ).astype(jnp.bfloat16)
    grad_up = jnp.einsum(
        "sxmf,sxmd->xfd", d_up, rows_in, preferred_element_type=jnp.float32
    ).astype(jnp.bfloat16)
    total = jnp.einsum("sxmf,xfd->sxmd", d_gate, w_gate, preferred_element_type=jnp.float32)
    expert_dx = lax.psum_scatter(
        (
            total + jnp.einsum("sxmf,xfd->sxmd", d_up, w_up, preferred_element_type=jnp.float32)
        ).astype(jnp.bfloat16),
        "dp",
        scatter_dimension=0,
        tiled=True,
    )
    back_dx = send_back(expert_dx[None])[0]
    out_slots = back_out.reshape(slot_total, model_width)
    dx_slots = back_dx.reshape(slot_total, model_width)
    per_choice = jnp.dot(selector.T, out_slots, preferred_element_type=jnp.float32)
    per_choice = per_choice.reshape(tok_rows, top_count, model_width)
    mixed = jnp.sum(router_probs[:, :, None] * per_choice, axis=1).astype(jnp.bfloat16)
    prob_grad = jnp.sum(out_grad.astype(jnp.float32)[:, None, :] * per_choice, axis=2)
    input_grad = jnp.dot(by_token.T, dx_slots, preferred_element_type=jnp.float32).astype(
        jnp.bfloat16
    )
    return (mixed, input_grad, prob_grad, grad_gate, grad_up, grad_down)


def solution(mesh):
    in_specs = (
        P(("dp", "expert"), None),
        P(("dp", "expert"), None),
        P(("dp", "expert"), None),
        P("expert", "dp", None),
        P("expert", "dp", None),
        P("expert", "dp", None),
        P(("dp", "expert"), None),
    )
    out_specs = (
        P(("dp", "expert"), None),
        P(("dp", "expert"), None),
        P(("dp", "expert"), None),
        P("expert", "dp", None),
        P("expert", "dp", None),
        P("expert", "dp", None),
    )
    return jax.shard_map(
        on_device, mesh=mesh, in_specs=in_specs, out_specs=out_specs, check_vma=False
    )
```

profile of v0, /device:TPU:1, one launch (start us, length us, event | category | flops | bytes accessed | tf_op | source)
XLA Modules:
  0.0 563.4 jit_solution(7334017989138479736)
XLA Ops:
  10.3 3.4 convolution_convert_fusion.1
  13.7 4.6 broadcast_in_dim_reshape.8
  18.3 59.5 %all_to_all.20 = bf16[1,32,1,9,4096]{4,3,2,0,1:T(8,128)(2,1)S(1)} all-to-all(bf16[1,32,1,9,4096]{4,3,2,0,1:T(8,128)(2,1)} %bitcast.143), channel_id=1, replica_groups=mesh['dp'=4,'expert'=32] {'expert'}, dimensions={1} | all-to-all | bytes 4718592 | tf_op jit(solution)/shard_map/all_to_all | solution.py:8
  81.9 4.1 broadcast_in_dim.22.clone
  86.0 6.3 %convert_element_type.98 = f32[256,4096]{1,0:T(8,128)} reshape(f32[128,2,4096]{2,1,0:T(2,128)} %broadcast_in_dim.22.clone) | data formatting | bytes 8388608 | tf_op jit(solution)/shard_map/convert_element_type | solution.py:40
  92.3 4.9 convolution_convert_fusion
  97.2 4.6 broadcast_in_dim_reshape.9
  101.8 55.1 %all_to_all.21 = bf16[1,32,1,9,4096]{4,3,2,0,1:T(8,128)(2,1)S(1)} all-to-all(bf16[1,32,1,9,4096]{4,3,2,0,1:T(8,128)(2,1)} %bitcast.144), channel_id=1, replica_groups=mesh['dp'=4,'expert'=32] {'expert'}, dimensions={1} | all-to-all | bytes 4718592 | tf_op jit(solution)/shard_map/all_to_all | solution.py:8
  160.2 11.2 %all-gather.5.cloned.1.call-done = bf16[4,32,1,9,4096]{4,1,3,2,0:T(8,128)(2,1)} async-done(((bf16[1,32,1,9,4096]{4,1,3,2,0:T(8,128)(2,1)}), bf16[4,32,1,9,4096]{4,1,3,2,0:T(8,128)(2,1)}) %all-gather.5.cloned.1.call-update) | async-done | bytes 9437200 | tf_op jit(solution)/shard_map/all_gather | solution.py:9
  171.4 8.7 %copy.79 = bf16[4,32,1,9,4096]{4,1,0,3,2:T(8,128)(2,1)} copy(bf16[4,32,1,9,4096]{4,1,3,2,0:T(8,128)(2,1)} %all-gather.5.cloned.1.call-done) | data formatting | bytes 18874368 | tf_op jit(solution)/shard_map/all_gather | solution.py:9
  180.1 8.9 %fusion.21 = f32[128,1,9,256]{3,0,2,1:T(8,128)} fusion(bf16[128,9,4096]{2,0,1:T(8,128)(2,1)} %bitcast.135, bf16[1,256,4096]{2,1,0:T(8,128)(2,1)} %param.11), kind=kOutput, calls=%fused_computation.30 | convolution fusion | flops 2415919104 | bytes 12713984 | tf_op jit(solution)/shard_map/sxmd,xfd->sxmf/dot_general | solution.py:47
  190.0 3.7 fusion.18
  193.7 72.4 %all-gather.7.cloned.1.call-done = bf16[4,32,1,9,4096]{4,1,3,2,0:T(8,128)(2,1)} async-done(((bf16[1,32,1,9,4096]{4,1,3,2,0:T(8,128)(2,1)}), bf16[4,32,1,9,4096]{4,1,3,2,0:T(8,128)(2,1)}) %all-gather.7.cloned.1.call-update) | async-done | bytes 9437200 | tf_op jit(solution)/shard_map/all_gather | solution.py:9
  266.1 8.8 %copy.86 = bf16[4,32,1,9,4096]{4,1,0,3,2:T(8,128)(2,1)} copy(bf16[4,32,1,9,4096]{4,1,3,2,0:T(8,128)(2,1)} %all-gather.7.cloned.1.call-done) | data formatting | bytes 18874368 | tf_op jit(solution)/shard_map/all_gather | solution.py:9
  274.9 8.4 %fusion.29 = (bf16[128,9,256]{2,0,1:T(8,128)(2,1)S(1)}, bf16[128,1,9,256]{3,0,2,1:T(8,128)(2,1)S(1)}, bf16[128,9,256]{2,0,1:T(8,128)(2,1)}) fusion(f32[128,1,9,256]{3,0,2,1:T(8,128)} %fusion.18, f32[128,1,9,256]{3,0,2,1:T(8,128)} %fusion.21, bf16[128,9,4096]{2,0,1:T(8,128)(2,1)} %bitcast.141, bf16[1,256,4096]{2,1,0:T(8,128)(2,1)S(1)} %copy-done), kind=kOutput, calls=%fused_computation.38 | convolution fusion | flops 2420342784 | bytes 15663104 | tf_op jit(solution)/shard_map/sxmd,xfd->sxmf/dot_general | solution.py:61
  283.2 8.3 %fusion.13 = f32[128,9,4096]{2,0,1:T(8,128)} fusion(bf16[1,256,4096]{2,1,0:T(8,128)(2,1)S(1)} %copy-done.9, bf16[128,1,9,256]{3,0,2,1:T(8,128)(2,1)S(1)} %get-tuple-element.9), kind=kOutput, calls=%fused_computation.24 | convolution fusion | flops 2415919104 | bytes 21561344 | tf_op jit(solution)/shard_map/sxmf,xfd->sxmd/dot_general | solution.py:75
  291.5 11.0 %fusion = bf16[128,1,9,4096]{3,0,2,1:T(8,128)(2,1)} fusion(f32[128,9,4096]{2,0,1:T(8,128)} %fusion.13, bf16[128,9,256]{2,0,1:T(8,128)(2,1)S(1)} %get-tuple-element.8, bf16[1,256,4096]{2,1,0:T(8,128)(2,1)} %param.11), kind=kOutput, calls=%fused_computation.1 | convolution fusion | flops 2425356288 | bytes 30998528 | tf_op jit(solution)/shard_map/sxmf,xfd->sxmd/dot_general | solution.py:78
  302.6 6.2 %convert_bitcast_fusion = bf16[128,1,9,4096]{3,0,2,1:T(8,128)(2,1)} fusion(bf16[128,9,256]{2,0,1:T(8,128)(2,1)} %get-tuple-element.10, bf16[1,256,4096]{2,1,0:T(8,128)(2,1)S(1)} %copy-done), kind=kOutput, calls=%fused_computation.2 | convolution fusion | flops 2420637696 | bytes 12124160 | tf_op jit(solution)/shard_map/sxmf,xfd->sxmd/dot_general | solution.py:52
  308.9 84.1 %reduce-scatter.5.cloned.1.call-done = bf16[32,1,9,4096]{3,0,2,1:T(8,128)(2,1)} async-done(((bf16[128,1,9,4096]{3,0,2,1:T(8,128)(2,1)}), bf16[32,1,9,4096]{3,0,2,1:T(8,128)(2,1)}) %reduce-scatter.5.cloned.1.call-update) | async-done | bytes 2359312 | tf_op jit(solution)/shard_map/reduce_scatter | solution.py:76
  393.0 5.1 copy.87
  398.1 7.5 %all-to-all-start.3 = ((bf16[1,32,1,9,4096]{4,3,2,0,1:T(8,128)(2,1)}), bf16[1,32,1,9,4096]{4,3,2,0,1:T(8,128)(2,1)}, u32[]{:S(2)}, u32[]{:S(2)}) async-start(bf16[1,32,1,9,4096]{4,3,2,0,1:T(8,128)(2,1)} %copy.87), calls=%async_computation.5 | async-start | bytes 8388608 | tf_op jit(solution)/shard_map/all_to_all | solution.py:14
  407.5 76.7 %reduce-scatter.3.cloned.1.call-done = bf16[32,1,9,4096]{3,0,2,1:T(8,128)(2,1)} async-done(((bf16[128,1,9,4096]{3,0,2,1:T(8,128)(2,1)}), bf16[32,1,9,4096]{3,0,2,1:T(8,128)(2,1)}) %reduce-scatter.3.cloned.1.call-update) | async-done | bytes 2359312 | tf_op jit(solution)/shard_map/reduce_scatter | solution.py:51
  484.1 5.1 copy.80
  489.3 7.7 %all-to-all-start.1 = ((bf16[1,32,1,9,4096]{4,3,2,0,1:T(8,128)(2,1)}), bf16[1,32,1,9,4096]{4,3,2,0,1:T(8,128)(2,1)}, u32[]{:S(2)}, u32[]{:S(2)}) async-start(bf16[1,32,1,9,4096]{4,3,2,0,1:T(8,128)(2,1)} %copy.80), calls=%async_computation.2 | async-start | bytes 8388608 | tf_op jit(solution)/shard_map/all_to_all | solution.py:14
  497.0 8.0 %fusion.4 = bf16[1,256,4096]{2,1,0:T(8,128)(2,1)} fusion(bf16[128,9,256]{2,0,1:T(8,128)(2,1)S(1)} %copy-done.5, bf16[128,9,4096]{2,0,1:T(8,128)(2,1)} %bitcast.142), kind=kOutput, calls=%fused_computation.11 | convolution fusion | flops 2416967680 | bytes 12124160 | tf_op jit(solution)/shard_map/sxmf,sxmd->xfd/dot_general | solution.py:62
  505.0 7.9 %fusion.5 = bf16[1,256,4096]{2,1,0:T(8,128)(2,1)} fusion(bf16[128,9,256]{2,0,1:T(8,128)(2,1)S(1)} %copy-done.7, bf16[128,9,4096]{2,0,1:T(8,128)(2,1)} %bitcast.136), kind=kOutput, calls=%fused_computation.12 | convolution fusion | flops 2416967680 | bytes 12124160 | tf_op jit(solution)/shard_map/sxmf,sxmd->xfd/dot_general | solution.py:72
  512.9 4.1 fusion.6
  517.0 4.7 reshape_squeeze.9
  521.7 3.4 convolution_convert_fusion.2
  525.1 22.1 %all-to-all-done.1 = bf16[1,32,1,9,4096]{4,3,2,0,1:T(8,128)(2,1)} async-done(((bf16[1,32,1,9,4096]{4,3,2,0,1:T(8,128)(2,1)}), bf16[1,32,1,9,4096]{4,3,2,0,1:T(8,128)(2,1)}, u32[]{:S(2)}, u32[]{:S(2)}) %all-to-all-start.1) | async-done | bytes 2359328 | tf_op jit(solution)/shard_map/all_to_all | solution.py:14
  547.1 4.7 reshape.153
  551.8 5.0 multiply_reduce_fusion
  (59 shorter events, 13.3 us)
Async XLA Ops:
  7.2 267.7 %copy-start = (bf16[1,256,4096]{2,1,0:T(8,128)(2,1)S(1)}, bf16[1,256,4096]{2,1,0:T(8,128)(2,1)}, u32[]{:S(2)}) copy-start(bf16[1,256,4096]{2,1,0:T(8,128)(2,1)} %param.12) | copy-start | bytes 6291460
  7.2 164.2 %all-gather.5.cloned.1.call-start = ((), (), s32[]{:S(2)}) async-start(), calls=%async_computation.8 | async-start | bytes 11796480 | tf_op jit(solution)/shard_map/all_gather | solution.py:9
  80.7 0.7 copy-start.10
  80.7 1.2 copy-start.2
  80.7 185.4 %all-gather.7.cloned.1.call-start = ((), (), s32[]{:S(2)}) async-start(), calls=%async_computation.9 | async-start | bytes 11796480 | tf_op jit(solution)/shard_map/all_gather | solution.py:9
  159.9 233.1 %reduce-scatter.5.cloned.1.call-start = ((), (), s32[]{:S(2)}) async-start(), calls=%async_computation.7 | async-start | bytes 11796480 | tf_op jit(solution)/shard_map/reduce_scatter | solution.py:76
  180.1 8.9 %copy-start.1 = (bf16[4,32,1,9,4096]{4,1,0,3,2:T(8,128)(2,1)S(1)}, bf16[4,32,1,9,4096]{4,1,0,3,2:T(8,128)(2,1)}, u32[]{:S(2)}) copy-start(bf16[4,32,1,9,4096]{4,1,0,3,2:T(8,128)(2,1)} %copy.79) | copy-start | bytes 28311556
  180.1 9.9 %copy-start.8 = (bf16[1,256,4096]{2,1,0:T(8,128)(2,1)S(1)}, bf16[1,256,4096]{2,1,0:T(8,128)(2,1)}, u32[]{:S(2)}) copy-start(bf16[1,256,4096]{2,1,0:T(8,128)(2,1)} %param.10) | copy-start | bytes 6291460
  274.9 8.4 %copy-start.9 = (bf16[1,256,4096]{2,1,0:T(8,128)(2,1)S(1)}, bf16[1,256,4096]{2,1,0:T(8,128)(2,1)}, u32[]{:S(2)}) copy-start(bf16[1,256,4096]{2,1,0:T(8,128)(2,1)} %param.10) | copy-start | bytes 6291460
  283.2 8.3 %copy-start.3 = (bf16[128,1,9,256]{3,0,2,1:T(8,128)(2,1)}, bf16[128,1,9,256]{3,0,2,1:T(8,128)(2,1)S(1)}, u32[]{:S(2)}) copy-start(bf16[128,1,9,256]{3,0,2,1:T(8,128)(2,1)S(1)} %get-tuple-element.9) | copy-start | bytes 1769476
  283.2 8.3 %copy-start.6 = (bf16[128,9,256]{2,0,1:T(8,128)(2,1)}, bf16[128,9,256]{2,0,1:T(8,128)(2,1)S(1)}, u32[]{:S(2)}) copy-start(bf16[128,9,256]{2,0,1:T(8,128)(2,1)S(1)} %get-tuple-element.8) | copy-start | bytes 1769476
  302.6 181.5 %reduce-scatter.3.cloned.1.call-start = ((), (), s32[]{:S(2)}) async-start(), calls=%async_computation.6 | async-start | bytes 11796480 | tf_op jit(solution)/shard_map/reduce_scatter | solution.py:51
  398.1 91.1 %all-to-all-start.3 = ((bf16[1,32,1,9,4096]{4,3,2,0,1:T(8,128)(2,1)}), bf16[1,32,1,9,4096]{4,3,2,0,1:T(8,128)(2,1)}, u32[]{:S(2)}, u32[]{:S(2)}) async-start(bf16[1,32,1,9,4096]{4,3,2,0,1:T(8,128)(2,1)} %copy.87), calls=%async_computation.5 | async-start | bytes 8388608 | tf_op jit(solution)/shard_map/all_to_all | solution.py:14
  489.3 7.7 %copy-start.5 = (bf16[128,9,256]{2,0,1:T(8,128)(2,1)S(1)}, bf16[128,9,256]{2,0,1:T(8,128)(2,1)}, u32[]{:S(2)}) copy-start(bf16[128,9,256]{2,0,1:T(8,128)(2,1)} %get-tuple-element.10) | copy-start | bytes 1769476
  489.3 57.8 %all-to-all-start.1 = ((bf16[1,32,1,9,4096]{4,3,2,0,1:T(8,128)(2,1)}), bf16[1,32,1,9,4096]{4,3,2,0,1:T(8,128)(2,1)}, u32[]{:S(2)}, u32[]{:S(2)}) async-start(bf16[1,32,1,9,4096]{4,3,2,0,1:T(8,128)(2,1)} %copy.80), calls=%async_computation.2 | async-start | bytes 8388608 | tf_op jit(solution)/shard_map/all_to_all | solution.py:14
  497.0 8.0 %copy-start.7 = (bf16[128,9,256]{2,0,1:T(8,128)(2,1)S(1)}, bf16[128,9,256]{2,0,1:T(8,128)(2,1)}, u32[]{:S(2)}) copy-start(bf16[128,9,256]{2,0,1:T(8,128)(2,1)} %copy-done.6) | copy-start | bytes 1769476
  497.0 15.9 %slice-start = ((s8[9437184]{0:T(1024)(128)(4,1)}), s8[4194304]{0:T(1024)(128)(4,1)S(1)}, s32[]{:S(2)}) async-start(s8[9437184]{0:T(1024)(128)(4,1)} %bitcast.138), calls=%async_computation.10 | async-start | bytes 8388608
  497.0 15.9 %slice-start.1 = ((s8[9437184]{0:T(1024)(128)(4,1)}), s8[4194304]{0:T(1024)(128)(4,1)S(1)}, s32[]{:S(2)}) async-start(s8[9437184]{0:T(1024)(128)(4,1)} %bitcast.138), calls=%async_computation.11 | async-start | bytes 8388608
  505.0 7.9 %slice-start.2 = ((s8[9437184]{0:T(1024)(128)(4,1)}), s8[1048576]{0:T(1024)(128)(4,1)S(1)}, s32[]{:S(2)}) async-start(s8[9437184]{0:T(1024)(128)(4,1)} %bitcast.138), calls=%async_computation.12 | async-start | bytes 2097152
  505.0 7.9 %copy-start.4 = (bf16[128,1,9,256]{3,0,2,1:T(8,128)(2,1)S(1)}, bf16[128,1,9,256]{3,0,2,1:T(8,128)(2,1)}, u32[]{:S(2)}) copy-start(bf16[128,1,9,256]{3,0,2,1:T(8,128)(2,1)} %copy-done.3) | copy-start | bytes 1769476
Sparse Core Ops, SparseCore 0:
  80.8 90.5 all-gather.4
  173.0 93.0 all-gather.6
  302.7 90.2 reduce-scatter.4
  395.3 88.7 reduce-scatter.2
where the time goes:
time: 567 us; the launch traced here: 563 us
  waiting for transfers between devices  267 us (47%)
  blocking collectives  115 us (20%)
  matrix products  83.1 us (15%)
  local copies, waits for them, and re-layouts  66.6 us (12%)
  starting transfers between devices  15.6 us (3%)
  between operations  13.9 us (2%)
    all_to_all x2, blocking collectives, deliver(): lax.all_to_all(stacked, 'expert', split_axis=1, concat_axis=1, tiled=True)  115 us
    reduce_scatter x1, waiting for transfers between devices, on_device(): lax.psum_scatter((total + jnp.einsum('sxmf,xfd->sxmd', d_up, w_up, prefer...  84.1 us
    all_gather x2, waiting for transfers between devices, deliver(): arrived = lax.all_gather(moved_rows[None], 'dp', axis=0, tiled=True)  83.7 us
    reduce_scatter x1, waiting for transfers between devices, on_device(): lax.psum_scatter(jnp.einsum('sxmf,xfd->sxmd', hidden, w_down, preferred_e...  76.7 us
    all_to_all x2, waiting for transfers between devices, send_back(): lax.all_to_all(stacked, 'expert', split_axis=1, concat_axis=1, tiled=True)  22.1 us
    all_gather x2, local copies, waits for them, and re-layouts, deliver(): arrived = lax.all_gather(moved_rows[None], 'dp', axis=0, tiled=True)  17.5 us
    all_to_all x2, starting transfers between devices, send_back(): lax.all_to_all(stacked, 'expert', split_axis=1, concat_axis=1, tiled=True)  15.2 us
  transfers between devices with their start and end apart: 6, of which 5 were waited for; matrix products, arithmetic and copies ran while one was open for 16% of the time, Pallas kernels for 0%

commit v1 on v0

--- a/solution.py
+++ b/solution.py
@@ -25,9 +25,9 @@
     slot_total = experts * slot_depth
     blocks = n_replica * n_expert
     flat_ids = expert_ids.reshape(-1)
-    onehot = (flat_ids[:, None] == jnp.arange(experts, dtype=jnp.int32)[None, :]).astype(jnp.int32)
-    earlier = jnp.cumsum(onehot, axis=0) - onehot
-    rank_of = jnp.sum(earlier * onehot, axis=1)
+    same = flat_ids[:, None] == flat_ids[None, :]
+    order = jnp.arange(flat_ids.shape[0], dtype=jnp.int32)
+    rank_of = jnp.sum((same & (order[None, :] < order[:, None])).astype(jnp.int32), axis=1)
     slot_of = flat_ids * slot_depth + rank_of
     selector = (jnp.arange(slot_total, dtype=jnp.int32)[:, None] == slot_of[None, :]).astype(
         jnp.bfloat16

time: 567 us -> 566 us (level)
  no operation moved by 1% of the time
where the time goes in v1:
time: 566 us; the launch traced here: 562 us
  waiting for transfers between devices  267 us (47%)
  blocking collectives  115 us (20%)
  matrix products  82.7 us (15%)
  local copies, waits for them, and re-layouts  66.3 us (12%)
  starting transfers between devices  15.6 us (3%)
  between operations  13.9 us (2%)
    all_to_all x2, blocking collectives, deliver(): lax.all_to_all(stacked, 'expert', split_axis=1, concat_axis=1, tiled=True)  115 us
    reduce_scatter x1, waiting for transfers between devices, on_device(): lax.psum_scatter((total + jnp.einsum('sxmf,xfd->sxmd', d_up, w_up, prefer...  84.3 us
    all_gather x2, waiting for transfers between devices, deliver(): arrived = lax.all_gather(moved_rows[None], 'dp', axis=0, tiled=True)  83.7 us
    reduce_scatter x1, waiting for transfers between devices, on_device(): lax.psum_scatter(jnp.einsum('sxmf,xfd->sxmd', hidden, w_down, preferred_e...  76.7 us
    all_to_all x2, waiting for transfers between devices, send_back(): lax.all_to_all(stacked, 'expert', split_axis=1, concat_axis=1, tiled=True)  22.1 us
    all_gather x2, local copies, waits for them, and re-layouts, deliver(): arrived = lax.all_gather(moved_rows[None], 'dp', axis=0, tiled=True)  17.5 us
    all_to_all x2, starting transfers between devices, send_back(): lax.all_to_all(stacked, 'expert', split_axis=1, concat_axis=1, tiled=True)  15.2 us
  transfers between devices with their start and end apart: 6, of which 5 were waited for; matrix products, arithmetic and copies ran while one was open for 16% of the time, Pallas kernels for 0%

profile of v1, /device:TPU:1, one launch (start us, length us, event | category | flops | bytes accessed | tf_op | source)
XLA Modules:
  0.0 562.4 jit_solution(3787388803330142517)
XLA Ops:
  9.4 3.5 convolution_convert_fusion.1
  12.9 4.7 broadcast_in_dim_reshape.4
  17.5 59.5 %all_to_all.20 = bf16[1,32,1,9,4096]{4,3,2,0,1:T(8,128)(2,1)S(1)} all-to-all(bf16[1,32,1,9,4096]{4,3,2,0,1:T(8,128)(2,1)} %bitcast.124), channel_id=1, replica_groups=mesh['dp'=4,'expert'=32] {'expert'}, dimensions={1} | all-to-all | bytes 4718592 | tf_op jit(solution)/shard_map/all_to_all | solution.py:8
  81.1 4.1 broadcast_in_dim.23.clone
  85.3 6.3 %convert_element_type.93 = f32[256,4096]{1,0:T(8,128)} reshape(f32[128,2,4096]{2,1,0:T(2,128)} %broadcast_in_dim.23.clone) | data formatting | bytes 8388608 | tf_op jit(solution)/shard_map/convert_element_type | solution.py:40
  91.6 4.8 convolution_convert_fusion
  96.4 4.6 broadcast_in_dim_reshape.10
  101.0 55.1 %all_to_all.21 = bf16[1,32,1,9,4096]{4,3,2,0,1:T(8,128)(2,1)S(1)} all-to-all(bf16[1,32,1,9,4096]{4,3,2,0,1:T(8,128)(2,1)} %bitcast.125), channel_id=1, replica_groups=mesh['dp'=4,'expert'=32] {'expert'}, dimensions={1} | all-to-all | bytes 4718592 | tf_op jit(solution)/shard_map/all_to_all | solution.py:8
  159.4 11.2 %all-gather.5.cloned.1.call-done = bf16[4,32,1,9,4096]{4,1,3,2,0:T(8,128)(2,1)} async-done(((bf16[1,32,1,9,4096]{4,1,3,2,0:T(8,128)(2,1)}), bf16[4,32,1,9,4096]{4,1,3,2,0:T(8,128)(2,1)}) %all-gather.5.cloned.1.call-update) | async-done | bytes 9437200 | tf_op jit(solution)/shard_map/all_gather | solution.py:9
  170.6 8.7 %copy.71 = bf16[4,32,1,9,4096]{4,1,0,3,2:T(8,128)(2,1)} copy(bf16[4,32,1,9,4096]{4,1,3,2,0:T(8,128)(2,1)} %all-gather.5.cloned.1.call-done) | data formatting | bytes 18874368 | tf_op jit(solution)/shard_map/all_gather | solution.py:9
  179.3 8.9 %fusion.21 = f32[128,1,9,256]{3,0,2,1:T(8,128)} fusion(bf16[128,9,4096]{2,0,1:T(8,128)(2,1)} %bitcast.116, bf16[1,256,4096]{2,1,0:T(8,128)(2,1)} %param.11), kind=kOutput, calls=%fused_computation.30 | convolution fusion | flops 2415919104 | bytes 12713984 | tf_op jit(solution)/shard_map/sxmd,xfd->sxmf/dot_general | solution.py:47
  189.2 3.7 fusion.18
  192.9 72.4 %all-gather.7.cloned.1.call-done = bf16[4,32,1,9,4096]{4,1,3,2,0:T(8,128)(2,1)} async-done(((bf16[1,32,1,9,4096]{4,1,3,2,0:T(8,128)(2,1)}), bf16[4,32,1,9,4096]{4,1,3,2,0:T(8,128)(2,1)}) %all-gather.7.cloned.1.call-update) | async-done | bytes 9437200 | tf_op jit(solution)/shard_map/all_gather | solution.py:9
  265.3 8.8 %copy.78 = bf16[4,32,1,9,4096]{4,1,0,3,2:T(8,128)(2,1)} copy(bf16[4,32,1,9,4096]{4,1,3,2,0:T(8,128)(2,1)} %all-gather.7.cloned.1.call-done) | data formatting | bytes 18874368 | tf_op jit(solution)/shard_map/all_gather | solution.py:9
  274.1 8.3 %fusion.29 = (bf16[128,9,256]{2,0,1:T(8,128)(2,1)S(1)}, bf16[128,1,9,256]{3,0,2,1:T(8,128)(2,1)S(1)}, bf16[128,9,256]{2,0,1:T(8,128)(2,1)}) fusion(f32[128,1,9,256]{3,0,2,1:T(8,128)} %fusion.18, f32[128,1,9,256]{3,0,2,1:T(8,128)} %fusion.21, bf16[128,9,4096]{2,0,1:T(8,128)(2,1)} %bitcast.122, bf16[1,256,4096]{2,1,0:T(8,128)(2,1)S(1)} %copy-done), kind=kOutput, calls=%fused_computation.38 | convolution fusion | flops 2420342784 | bytes 15663104 | tf_op jit(solution)/shard_map/sxmd,xfd->sxmf/dot_general | solution.py:61
  282.5 8.0 %fusion.13 = f32[128,9,4096]{2,0,1:T(8,128)} fusion(bf16[1,256,4096]{2,1,0:T(8,128)(2,1)S(1)} %copy-done.9, bf16[128,1,9,256]{3,0,2,1:T(8,128)(2,1)S(1)} %get-tuple-element.9), kind=kOutput, calls=%fused_computation.24 | convolution fusion | flops 2415919104 | bytes 21561344 | tf_op jit(solution)/shard_map/sxmf,xfd->sxmd/dot_general | solution.py:75
  290.5 11.1 %fusion = bf16[128,1,9,4096]{3,0,2,1:T(8,128)(2,1)} fusion(f32[128,9,4096]{2,0,1:T(8,128)} %fusion.13, bf16[128,9,256]{2,0,1:T(8,128)(2,1)S(1)} %get-tuple-element.8, bf16[1,256,4096]{2,1,0:T(8,128)(2,1)} %param.11), kind=kOutput, calls=%fused_computation.1 | convolution fusion | flops 2425356288 | bytes 30998528 | tf_op jit(solution)/shard_map/sxmf,xfd->sxmd/dot_general | solution.py:78
  301.6 6.0 %convert_bitcast_fusion = bf16[128,1,9,4096]{3,0,2,1:T(8,128)(2,1)} fusion(bf16[128,9,256]{2,0,1:T(8,128)(2,1)} %get-tuple-element.10, bf16[1,256,4096]{2,1,0:T(8,128)(2,1)S(1)} %copy-done), kind=kOutput, calls=%fused_computation.2 | convolution fusion | flops 2420637696 | bytes 12124160 | tf_op jit(solution)/shard_map/sxmf,xfd->sxmd/dot_general | solution.py:52
  307.7 84.3 %reduce-scatter.5.cloned.1.call-done = bf16[32,1,9,4096]{3,0,2,1:T(8,128)(2,1)} async-done(((bf16[128,1,9,4096]{3,0,2,1:T(8,128)(2,1)}), bf16[32,1,9,4096]{3,0,2,1:T(8,128)(2,1)}) %reduce-scatter.5.cloned.1.call-update) | async-done | bytes 2359312 | tf_op jit(solution)/shard_map/reduce_scatter | solution.py:76
  392.0 5.1 copy.79
  397.1 7.5 %all-to-all-start.3 = ((bf16[1,32,1,9,4096]{4,3,2,0,1:T(8,128)(2,1)}), bf16[1,32,1,9,4096]{4,3,2,0,1:T(8,128)(2,1)}, u32[]{:S(2)}, u32[]{:S(2)}) async-start(bf16[1,32,1,9,4096]{4,3,2,0,1:T(8,128)(2,1)} %copy.79), calls=%async_computation.5 | async-start | bytes 8388608 | tf_op jit(solution)/shard_map/all_to_all | solution.py:14
  406.4 76.7 %reduce-scatter.3.cloned.1.call-done = bf16[32,1,9,4096]{3,0,2,1:T(8,128)(2,1)} async-done(((bf16[128,1,9,4096]{3,0,2,1:T(8,128)(2,1)}), bf16[32,1,9,4096]{3,0,2,1:T(8,128)(2,1)}) %reduce-scatter.3.cloned.1.call-update) | async-done | bytes 2359312 | tf_op jit(solution)/shard_map/reduce_scatter | solution.py:51
  483.1 5.1 copy.72
  488.3 7.7 %all-to-all-start.1 = ((bf16[1,32,1,9,4096]{4,3,2,0,1:T(8,128)(2,1)}), bf16[1,32,1,9,4096]{4,3,2,0,1:T(8,128)(2,1)}, u32[]{:S(2)}, u32[]{:S(2)}) async-start(bf16[1,32,1,9,4096]{4,3,2,0,1:T(8,128)(2,1)} %copy.72), calls=%async_computation.2 | async-start | bytes 8388608 | tf_op jit(solution)/shard_map/all_to_all | solution.py:14
  496.0 8.0 %fusion.4 = bf16[1,256,4096]{2,1,0:T(8,128)(2,1)} fusion(bf16[128,9,256]{2,0,1:T(8,128)(2,1)S(1)} %copy-done.5, bf16[128,9,4096]{2,0,1:T(8,128)(2,1)} %bitcast.123), kind=kOutput, calls=%fused_computation.11 | convolution fusion | flops 2416967680 | bytes 12124160 | tf_op jit(solution)/shard_map/sxmf,sxmd->xfd/dot_general | solution.py:62
  504.0 7.9 %fusion.5 = bf16[1,256,4096]{2,1,0:T(8,128)(2,1)} fusion(bf16[128,9,256]{2,0,1:T(8,128)(2,1)S(1)} %copy-done.7, bf16[128,9,4096]{2,0,1:T(8,128)(2,1)} %bitcast.117), kind=kOutput, calls=%fused_computation.12 | convolution fusion | flops 2416967680 | bytes 12124160 | tf_op jit(solution)/shard_map/sxmf,sxmd->xfd/dot_general | solution.py:72
  512.0 4.1 fusion.6
  516.0 4.7 reshape_squeeze.9
  520.7 3.4 convolution_convert_fusion.2
  524.1 22.1 %all-to-all-done.1 = bf16[1,32,1,9,4096]{4,3,2,0,1:T(8,128)(2,1)} async-done(((bf16[1,32,1,9,4096]{4,3,2,0,1:T(8,128)(2,1)}), bf16[1,32,1,9,4096]{4,3,2,0,1:T(8,128)(2,1)}, u32[]{:S(2)}, u32[]{:S(2)}) %all-to-all-start.1) | async-done | bytes 2359328 | tf_op jit(solution)/shard_map/all_to_all | solution.py:14
  546.1 4.7 reshape.137
  550.8 5.1 multiply_reduce_fusion
  (53 shorter events, 12.4 us)
Async XLA Ops:
  7.2 266.9 %copy-start = (bf16[1,256,4096]{2,1,0:T(8,128)(2,1)S(1)}, bf16[1,256,4096]{2,1,0:T(8,128)(2,1)}, u32[]{:S(2)}) copy-start(bf16[1,256,4096]{2,1,0:T(8,128)(2,1)} %param.12) | copy-start | bytes 6291460
  7.2 163.4 %all-gather.5.cloned.1.call-start = ((), (), s32[]{:S(2)}) async-start(), calls=%async_computation.8 | async-start | bytes 11796480 | tf_op jit(solution)/shard_map/all_gather | solution.py:9
  79.9 0.7 copy-start.10
  79.9 1.2 copy-start.2
  79.9 185.4 %all-gather.7.cloned.1.call-start = ((), (), s32[]{:S(2)}) async-start(), calls=%async_computation.9 | async-start | bytes 11796480 | tf_op jit(solution)/shard_map/all_gather | solution.py:9
  159.1 232.9 %reduce-scatter.5.cloned.1.call-start = ((), (), s32[]{:S(2)}) async-start(), calls=%async_computation.7 | async-start | bytes 11796480 | tf_op jit(solution)/shard_map/reduce_scatter | solution.py:76
  179.3 8.9 %copy-start.1 = (bf16[4,32,1,9,4096]{4,1,0,3,2:T(8,128)(2,1)S(1)}, bf16[4,32,1,9,4096]{4,1,0,3,2:T(8,128)(2,1)}, u32[]{:S(2)}) copy-start(bf16[4,32,1,9,4096]{4,1,0,3,2:T(8,128)(2,1)} %copy.71) | copy-start | bytes 28311556
  179.3 9.9 %copy-start.8 = (bf16[1,256,4096]{2,1,0:T(8,128)(2,1)S(1)}, bf16[1,256,4096]{2,1,0:T(8,128)(2,1)}, u32[]{:S(2)}) copy-start(bf16[1,256,4096]{2,1,0:T(8,128)(2,1)} %param.10) | copy-start | bytes 6291460
  274.1 8.4 %copy-start.9 = (bf16[1,256,4096]{2,1,0:T(8,128)(2,1)S(1)}, bf16[1,256,4096]{2,1,0:T(8,128)(2,1)}, u32[]{:S(2)}) copy-start(bf16[1,256,4096]{2,1,0:T(8,128)(2,1)} %param.10) | copy-start | bytes 6291460
  282.5 8.0 %copy-start.3 = (bf16[128,1,9,256]{3,0,2,1:T(8,128)(2,1)}, bf16[128,1,9,256]{3,0,2,1:T(8,128)(2,1)S(1)}, u32[]{:S(2)}) copy-start(bf16[128,1,9,256]{3,0,2,1:T(8,128)(2,1)S(1)} %get-tuple-element.9) | copy-start | bytes 1769476
  282.5 8.0 %copy-start.6 = (bf16[128,9,256]{2,0,1:T(8,128)(2,1)}, bf16[128,9,256]{2,0,1:T(8,128)(2,1)S(1)}, u32[]{:S(2)}) copy-start(bf16[128,9,256]{2,0,1:T(8,128)(2,1)S(1)} %get-tuple-element.8) | copy-start | bytes 1769476
  301.6 181.5 %reduce-scatter.3.cloned.1.call-start = ((), (), s32[]{:S(2)}) async-start(), calls=%async_computation.6 | async-start | bytes 11796480 | tf_op jit(solution)/shard_map/reduce_scatter | solution.py:51
  397.1 91.2 %all-to-all-start.3 = ((bf16[1,32,1,9,4096]{4,3,2,0,1:T(8,128)(2,1)}), bf16[1,32,1,9,4096]{4,3,2,0,1:T(8,128)(2,1)}, u32[]{:S(2)}, u32[]{:S(2)}) async-start(bf16[1,32,1,9,4096]{4,3,2,0,1:T(8,128)(2,1)} %copy.79), calls=%async_computation.5 | async-start | bytes 8388608 | tf_op jit(solution)/shard_map/all_to_all | solution.py:14
  488.3 7.7 %copy-start.5 = (bf16[128,9,256]{2,0,1:T(8,128)(2,1)S(1)}, bf16[128,9,256]{2,0,1:T(8,128)(2,1)}, u32[]{:S(2)}) copy-start(bf16[128,9,256]{2,0,1:T(8,128)(2,1)} %get-tuple-element.10) | copy-start | bytes 1769476
  488.3 57.8 %all-to-all-start.1 = ((bf16[1,32,1,9,4096]{4,3,2,0,1:T(8,128)(2,1)}), bf16[1,32,1,9,4096]{4,3,2,0,1:T(8,128)(2,1)}, u32[]{:S(2)}, u32[]{:S(2)}) async-start(bf16[1,32,1,9,4096]{4,3,2,0,1:T(8,128)(2,1)} %copy.72), calls=%async_computation.2 | async-start | bytes 8388608 | tf_op jit(solution)/shard_map/all_to_all | solution.py:14
  496.0 8.0 %copy-start.7 = (bf16[128,9,256]{2,0,1:T(8,128)(2,1)S(1)}, bf16[128,9,256]{2,0,1:T(8,128)(2,1)}, u32[]{:S(2)}) copy-start(bf16[128,9,256]{2,0,1:T(8,128)(2,1)} %copy-done.6) | copy-start | bytes 1769476
  496.0 15.9 %slice-start = ((s8[9437184]{0:T(1024)(128)(4,1)}), s8[4194304]{0:T(1024)(128)(4,1)S(1)}, s32[]{:S(2)}) async-start(s8[9437184]{0:T(1024)(128)(4,1)} %bitcast.119), calls=%async_computation.10 | async-start | bytes 8388608
  496.0 15.9 %slice-start.1 = ((s8[9437184]{0:T(1024)(128)(4,1)}), s8[4194304]{0:T(1024)(128)(4,1)S(1)}, s32[]{:S(2)}) async-start(s8[9437184]{0:T(1024)(128)(4,1)} %bitcast.119), calls=%async_computation.11 | async-start | bytes 8388608
  504.0 7.9 %slice-start.2 = ((s8[9437184]{0:T(1024)(128)(4,1)}), s8[1048576]{0:T(1024)(128)(4,1)S(1)}, s32[]{:S(2)}) async-start(s8[9437184]{0:T(1024)(128)(4,1)} %bitcast.119), calls=%async_computation.12 | async-start | bytes 2097152
  504.0 7.9 %copy-start.4 = (bf16[128,1,9,256]{3,0,2,1:T(8,128)(2,1)S(1)}, bf16[128,1,9,256]{3,0,2,1:T(8,128)(2,1)}, u32[]{:S(2)}) copy-start(bf16[128,1,9,256]{3,0,2,1:T(8,128)(2,1)} %copy-done.3) | copy-start | bytes 1769476
Sparse Core Ops, SparseCore 0:
  80.0 90.5 all-gather.4
  172.3 93.0 all-gather.6
  301.7 90.2 reduce-scatter.4
  394.3 88.7 reduce-scatter.2

commit v2 on v1

v2 whole, which is shorter than its diff:
```python
import jax
import jax.numpy as jnp
from jax import lax
from jax.sharding import PartitionSpec as P

AXES = ("dp", "expert")
F32 = jnp.float32
BF16 = jnp.bfloat16


def pairings(n_dp, n_expert):
    first, second = [], []
    for z in range(n_dp):
        near, far = z ^ 1, n_dp - 1 - z
        for e in range(n_expert):
            a, b = (near, far) if e % 2 == 0 else (far, near)
            first.append((z * n_expert + e, a * n_expert + e))
            second.append((z * n_expert + e, b * n_expert + e))
    return first, second


def exchange(rows, n_expert):
    total, width = rows.shape
    packed = rows.reshape(n_expert, total // n_expert * (width // 128), 128)
    moved = lax.all_to_all(packed, "expert", split_axis=0, concat_axis=0, tiled=True)
    return moved.reshape(total, width)


def nt(a, b):
    return lax.dot_general(a, b, (((1,), (1,)), ((), ())), preferred_element_type=F32)


def tn(a, b):
    return lax.dot_general(a, b, (((0,), (0,)), ((), ())), preferred_element_type=F32)


def nn(a, b):
    return jnp.dot(a, b, preferred_element_type=F32)


def on_device(tokens, expert_ids, router_probs, w_gate, w_up, w_down, out_grad):
    tok_rows, model_width = tokens.shape
    top_count = expert_ids.shape[1]
    n_expert = lax.axis_size("expert")
    n_dp = lax.axis_size("dp")
    depth = 9
    slots = n_expert * depth
    quarter = w_gate.shape[1]
    row_pairs, weight_pairs = pairings(n_dp, n_expert)

    def swap_rows(x):
        return lax.ppermute(x, AXES, row_pairs)

    def swap_weights(x):
        return lax.ppermute(x, AXES, weight_pairs)

    gate_w = jnp.concatenate([w_gate[0], swap_weights(w_gate[0])], axis=0)
    up_w = jnp.concatenate([w_up[0], swap_weights(w_up[0])], axis=0)
    down_w = jnp.concatenate([w_down[0], swap_weights(w_down[0])], axis=0)

    flat_ids = expert_ids.reshape(-1)
    same = flat_ids[:, None] == flat_ids[None, :]
    order = jnp.arange(flat_ids.shape[0], dtype=jnp.int32)
    rank_of = jnp.sum((same & (order[None, :] < order[:, None])).astype(jnp.int32), axis=1)
    slot_of = flat_ids * depth + rank_of
    selector = (jnp.arange(slots, dtype=jnp.int32)[:, None] == slot_of[None, :]).astype(BF16)
    by_token = jnp.sum(selector.reshape(slots, tok_rows, top_count), axis=2)

    send_tokens = nn(by_token, tokens).astype(BF16)
    mine = exchange(send_tokens, n_expert)
    theirs = swap_rows(mine)
    scaled = (
        router_probs.reshape(-1)[:, None] * jnp.repeat(out_grad, top_count, axis=0).astype(F32)
    ).astype(BF16)
    send_grads = nn(selector, scaled).astype(BF16)
    mine_g = exchange(send_grads, n_expert)
    theirs_g = swap_rows(mine_g)

    rows = jnp.concatenate([mine, theirs], axis=0)
    grads = jnp.concatenate([mine_g, theirs_g], axis=0)
    gate_proj = nt(rows, gate_w)
    up_proj = nt(rows, up_w)
    sig = jax.nn.sigmoid(gate_proj)
    activated = gate_proj * sig
    hidden = (activated * up_proj).astype(BF16)

    out_theirs = swap_rows(nn(hidden[slots:], down_w).astype(BF16))
    out_rows = (nn(hidden[:slots], down_w) + out_theirs.astype(F32)).astype(BF16)
    back_out = exchange(out_rows, n_expert)

    d_hidden = nt(grads, down_w)
    d_gate = (d_hidden * up_proj * sig * (1.0 + gate_proj * (1.0 - sig))).astype(BF16)
    d_up = (d_hidden * activated).astype(BF16)
    dx_theirs = swap_rows((nn(d_gate[slots:], gate_w) + nn(d_up[slots:], up_w)).astype(BF16))
    dx_rows = (
        nn(d_gate[:slots], gate_w) + nn(d_up[:slots], up_w) + dx_theirs.astype(F32)
    ).astype(BF16)
    back_dx = exchange(dx_rows, n_expert)

    def reduced(units, data):
        other = swap_weights(tn(units[:, quarter:], data).astype(BF16))
        return (tn(units[:, :quarter], data) + other.astype(F32)).astype(BF16)[None]

    grad_down = reduced(hidden, grads)
    grad_gate = reduced(d_gate, rows)
    grad_up = reduced(d_up, rows)

    per_choice = tn(selector, back_out).reshape(tok_rows, top_count, model_width)
    mixed = jnp.sum(router_probs[:, :, None] * per_choice, axis=1).astype(BF16)
    prob_grad = jnp.sum(out_grad.astype(F32)[:, None, :] * per_choice, axis=2)
    input_grad = tn(by_token, back_dx).astype(BF16)
    return (mixed, input_grad, prob_grad, grad_gate, grad_up, grad_down)


def solution(mesh):
    rows = P(("dp", "expert"), None)
    weights = P("expert", "dp", None)
    return jax.shard_map(
        on_device,
        mesh=mesh,
        in_specs=(rows, rows, rows, weights, weights, weights, rows),
        out_specs=(rows, rows, rows, weights, weights, weights),
        check_vma=False,
    )
```

time: 566 us -> 340 us (0.60)
  blocking collectives: 115 us -> 0 us
  waiting for transfers between devices: 267 us -> 181 us
  starting transfers between devices: 15.6 us -> 41.7 us
  matrix products: 82.7 us -> 60.3 us
  local copies, waits for them, and re-layouts: 66.3 us -> 46.1 us
  between operations: 13.9 us -> 1.4 us
    reduce_scatter x2 -> x0, waiting for transfers between devices: 161 us -> none  [the longest x1 84.3 us: on_device(): lax.psum_scatter((total + jnp.einsum('sxmf,xfd->sxmd', d_up, w_up, prefer...]
    ppermute x0 -> x10, waiting for transfers between devices: none -> 136 us  [the longest x6 68.7 us: swap_weights(): return lax.ppermute(x, AXES, weight_pairs)]
    all_to_all x2 -> x0, blocking collectives: 115 us -> none  [deliver(): lax.all_to_all(stacked, 'expert', split_axis=1, concat_axis=1, tiled=True)]
    all_gather x2 -> x0, waiting for transfers between devices: 83.7 us -> none  [deliver(): arrived = lax.all_gather(moved_rows[None], 'dp', axis=0, tiled=True)]
    reshape x0 -> x8, local copies, waits for them, and re-layouts: none -> 31 us  [the longest x4 16 us: exchange(): return moved.reshape(total, width)]
    all_to_all x2 -> x4, waiting for transfers between devices: 22.1 us -> 45 us  [exchange(): lax.all_to_all(packed, 'expert', split_axis=0, concat_axis=0, tiled=True)]
    dot_general x13 -> x19, matrix products: 82.7 us -> 60.3 us  [the longest x8 34 us: tn(): lax.dot_general(a, b, (((0,), (0,)), ((), ())), preferred_element_type=F32)]
    another operation x4 -> x0, local copies, waits for them, and re-layouts: 18.7 us -> none  [the longest x1 4.69 us: on_device(): out_slots = back_out.reshape(slot_total, model_width)]
  transfers between devices with their start and end apart: 6 -> 14, of which waited for: 5 -> 10; matrix products, arithmetic and copies ran while one was open for 16% -> 27% of each run, Pallas kernels for 0% -> 0%
where the time goes in v2:
time: 340 us; the launch traced here: 333 us
  waiting for transfers between devices  181 us (53%)
  matrix products  60.3 us (18%)
  local copies, waits for them, and re-layouts  46.1 us (14%)
  starting transfers between devices  41.7 us (12%)
    ppermute x6, waiting for transfers between devices, swap_weights(): return lax.ppermute(x, AXES, weight_pairs)  68.7 us
    ppermute x4, waiting for transfers between devices, swap_rows(): return lax.ppermute(x, AXES, row_pairs)  67.4 us
    all_to_all x4, waiting for transfers between devices, exchange(): lax.all_to_all(packed, 'expert', split_axis=0, concat_axis=0, tiled=True)  45 us
    dot_general x8, matrix products, tn(): lax.dot_general(a, b, (((0,), (0,)), ((), ())), preferred_element_type=F32)  34 us
    all_to_all x4, starting transfers between devices, exchange(): lax.all_to_all(packed, 'expert', split_axis=0, concat_axis=0, tiled=True)  28 us
    dot_general x8, matrix products, nn(): return jnp.dot(a, b, preferred_element_type=F32)  17.9 us
    reshape x4, local copies, waits for them, and re-layouts, exchange(): return moved.reshape(total, width)  16 us
    reshape x4, local copies, waits for them, and re-layouts, exchange(): packed = rows.reshape(n_expert, total // n_expert * (width // 128), 128)  15 us
  transfers between devices with their start and end apart: 14, of which 10 were waited for; matrix products, arithmetic and copies ran while one was open for 27% of the time, Pallas kernels for 0%

profile of v2, /device:TPU:1, one launch (start us, length us, event | category | flops | bytes accessed | tf_op | source)
XLA Modules:
  0.0 333.2 jit_solution(15579261838044632616)
XLA Ops:
  6.1 8.6 %all-to-all-start = ((bf16[32,288,128]{2,1,0:T(8,128)(2,1)}), bf16[32,288,128]{2,1,0:T(8,128)(2,1)}, u32[]{:S(2)}, u32[]{:S(2)}) async-start(bf16[32,288,128]{2,1,0:T(8,128)(2,1)} %reshape.91), calls=%async_computation | async-start | bytes 4718592 | tf_op jit(solution)/shard_map/all_to_all | solution.py:25
  14.8 4.1 %broadcast_in_dim.8.clone = f32[128,2,4096]{2,1,0:T(2,128)} broadcast(bf16[128,4096]{1,0:T(8,128)(2,1)S(1)} %copy-done.5), dimensions={0,2} | broadcast | bytes 5242880 | tf_op jit(solution)/shard_map/broadcast_in_dim | solution.py:73
  18.9 6.2 %convert_element_type.95 = f32[256,4096]{1,0:T(8,128)} reshape(f32[128,2,4096]{2,1,0:T(2,128)} %broadcast_in_dim.8.clone) | data formatting | bytes 8388608 | tf_op jit(solution)/shard_map/convert_element_type | solution.py:73
  30.8 14.8 %all-to-all-done = bf16[32,288,128]{2,1,0:T(8,128)(2,1)} async-done(((bf16[32,288,128]{2,1,0:T(8,128)(2,1)}), bf16[32,288,128]{2,1,0:T(8,128)(2,1)}, u32[]{:S(2)}, u32[]{:S(2)}) %all-to-all-start) | async-done | bytes 2359328 | tf_op jit(solution)/shard_map/all_to_all | solution.py:25
  45.6 7.0 %all-to-all-start.2 = ((bf16[32,288,128]{2,1,0:T(8,128)(2,1)}), bf16[32,288,128]{2,1,0:T(8,128)(2,1)}, u32[]{:S(2)}, u32[]{:S(2)}) async-start(bf16[32,288,128]{2,1,0:T(8,128)(2,1)} %reshape.95), calls=%async_computation.2 | async-start | bytes 4718592 | tf_op jit(solution)/shard_map/all_to_all | solution.py:25
  52.6 3.7 %reshape.92 = bf16[288,4096]{1,0:T(8,128)(2,1)S(1)} reshape(bf16[32,288,128]{2,1,0:T(8,128)(2,1)} %all-to-all-done) | data formatting | bytes 4718592 | tf_op jit(solution)/shard_map/reshape | solution.py:26
  56.2 3.8 %collective-permute-start = (bf16[288,4096]{1,0:T(8,128)(2,1)S(1)}, bf16[288,4096]{1,0:T(8,128)(2,1)}, u32[]{:S(2)}, u32[]{:S(2)}) collective-permute-start(bf16[288,4096]{1,0:T(8,128)(2,1)S(1)} %reshape.92), channel_id=1, source_target_pairs={{0,32},{1,97},{2,34},{3,99},{4,36},{5,101},{6,38},{7,103},{8,40},{... | collective-permute-start | bytes 7077896 | tf_op jit(solution)/shard_map/ppermute | solution.py:52
  60.1 23.4 %all-to-all-done.2 = bf16[32,288,128]{2,1,0:T(8,128)(2,1)} async-done(((bf16[32,288,128]{2,1,0:T(8,128)(2,1)}), bf16[32,288,128]{2,1,0:T(8,128)(2,1)}, u32[]{:S(2)}, u32[]{:S(2)}) %all-to-all-start.2) | async-done | bytes 2359328 | tf_op jit(solution)/shard_map/all_to_all | solution.py:25
  83.4 4.9 %reshape.96 = bf16[288,4096]{1,0:T(8,128)(2,1)} reshape(bf16[32,288,128]{2,1,0:T(8,128)(2,1)} %all-to-all-done.2) | data formatting | bytes 4718592 | tf_op jit(solution)/shard_map/reshape | solution.py:26
  88.4 3.8 %collective-permute-start.5 = (bf16[288,4096]{1,0:T(8,128)(2,1)}, bf16[288,4096]{1,0:T(8,128)(2,1)S(1)}, u32[]{:S(2)}, u32[]{:S(2)}) collective-permute-start(bf16[288,4096]{1,0:T(8,128)(2,1)} %reshape.96), channel_id=1, source_target_pairs={{0,32},{1,97},{2,34},{3,99},{4,36},{5,101},{6,38},{7,103},{8,40},{... | collective-permute-start | bytes 7077896 | tf_op jit(solution)/shard_map/ppermute | solution.py:52
  96.2 44.1 %collective-permute-done.5 = bf16[288,4096]{1,0:T(8,128)(2,1)S(1)} collective-permute-done((bf16[288,4096]{1,0:T(8,128)(2,1)}, bf16[288,4096]{1,0:T(8,128)(2,1)S(1)}, u32[]{:S(2)}, u32[]{:S(2)}) %collective-permute-start.5) | collective-permute-done | bytes 2359328 | tf_op jit(solution)/shard_map/ppermute | solution.py:52
  143.2 21.5 %collective-permute-done.3 = bf16[256,4096]{1,0:T(8,128)(2,1)S(1)} collective-permute-done((bf16[256,4096]{1,0:T(8,128)(2,1)}, bf16[256,4096]{1,0:T(8,128)(2,1)S(1)}, u32[]{:S(2)}, u32[]{:S(2)}) %collective-permute-start.3) | collective-permute-done | bytes 2097184 | tf_op jit(solution)/shard_map/ppermute | solution.py:55
  167.3 19.5 %collective-permute-done.1 = bf16[256,4096]{1,0:T(8,128)(2,1)S(1)} collective-permute-done((bf16[256,4096]{1,0:T(8,128)(2,1)}, bf16[256,4096]{1,0:T(8,128)(2,1)S(1)}, u32[]{:S(2)}, u32[]{:S(2)}) %collective-permute-start.1) | collective-permute-done | bytes 2097184 | tf_op jit(solution)/shard_map/ppermute | solution.py:55
  186.8 3.1 multiply_convert_fusion.3
  200.3 21.7 %collective-permute-done.6 = bf16[288,4096]{1,0:T(8,128)(2,1)S(1)} collective-permute-done((bf16[288,4096]{1,0:T(8,128)(2,1)S(1)}, bf16[288,4096]{1,0:T(8,128)(2,1)S(1)}, u32[]{:S(2)}, u32[]{:S(2)}) %collective-permute-start.6) | collective-permute-done | bytes 2359328 | tf_op jit(solution)/shard_map/ppermute | solution.py:52
  224.8 5.0 %reshape.97 = bf16[32,288,128]{2,1,0:T(8,128)(2,1)} reshape(bf16[288,4096]{1,0:T(8,128)(2,1)} %fusion.1) | data formatting | bytes 4718592 | tf_op jit(solution)/shard_map/reshape | solution.py:24
  229.8 5.0 %all-to-all-start.3 = ((bf16[32,288,128]{2,1,0:T(8,128)(2,1)}), bf16[32,288,128]{2,1,0:T(8,128)(2,1)}, u32[]{:S(2)}, u32[]{:S(2)}) async-start(bf16[32,288,128]{2,1,0:T(8,128)(2,1)} %reshape.97), calls=%async_computation.3 | async-start | bytes 4718592 | tf_op jit(solution)/shard_map/all_to_all | solution.py:25
  234.9 5.7 %convolution_convert_fusion.3 = bf16[256,4096]{1,0:T(8,128)(2,1)} fusion(bf16[576,4096]{1,0:T(8,128)(2,1)} %copy-done.3, bf16[576,512]{1,0:T(8,128)(2,1)S(1)} %get-tuple-element.10), kind=kOutput, calls=%fused_computation.16 | convolution fusion | flops 1209008128 | bytes 7110656 | tf_op jit(solution)/shard_map/dot_general | solution.py:34
  240.6 3.1 convolution_convert_fusion.4
  245.2 3.1 convolution_convert_fusion.5
  249.9 3.9 %fusion.2 = bf16[288,4096]{1,0:T(8,128)(2,1)} fusion(bf16[288,4096]{1,0:T(8,128)(2,1)} %collective-permute-done.4, bf16[256,4096]{1,0:T(8,128)(2,1)S(1)} %copy-done.12, bf16[256,4096]{1,0:T(8,128)(2,1)S(1)} %bitcast.38, bf16[576,512]{1,0:T(8,128)(2,1)S(1)} %get-tuple-element.10), kind=kOutput, calls=%fused_computation.5 | convolution fusion | flops 1219887104 | bytes 9207808 | tf_op jit(solution)/shard_map/dot_general | solution.py:38
  253.8 5.0 %reshape.93 = bf16[32,288,128]{2,1,0:T(8,128)(2,1)} reshape(bf16[288,4096]{1,0:T(8,128)(2,1)} %fusion.2) | data formatting | bytes 4718592 | tf_op jit(solution)/shard_map/reshape | solution.py:24
  258.8 6.8 %all-to-all-done.3 = bf16[32,288,128]{2,1,0:T(8,128)(2,1)} async-done(((bf16[32,288,128]{2,1,0:T(8,128)(2,1)}), bf16[32,288,128]{2,1,0:T(8,128)(2,1)}, u32[]{:S(2)}, u32[]{:S(2)}) %all-to-all-start.3) | async-done | bytes 2359328 | tf_op jit(solution)/shard_map/all_to_all | solution.py:25
  265.7 7.4 %all-to-all-start.1 = ((bf16[32,288,128]{2,1,0:T(8,128)(2,1)}), bf16[32,288,128]{2,1,0:T(8,128)(2,1)}, u32[]{:S(2)}, u32[]{:S(2)}) async-start(bf16[32,288,128]{2,1,0:T(8,128)(2,1)} %reshape.93), calls=%async_computation.1 | async-start | bytes 4718592 | tf_op jit(solution)/shard_map/all_to_all | solution.py:25
  275.5 6.3 %fusion.7 = bf16[1,256,4096]{2,1,0:T(8,128)(2,1)} fusion(bf16[576,4096]{1,0:T(8,128)(2,1)} %copy-done.3, bf16[256,4096]{1,0:T(8,128)(2,1)} %collective-permute-done.9, bf16[576,512]{1,0:T(8,128)(2,1)S(1)} %get-tuple-element.10), kind=kOutput, calls=%fused_computation.19 | convolution fusion | flops 1211105280 | bytes 9207808 | tf_op jit(solution)/shard_map/dot_general | solution.py:34
  281.8 10.1 %collective-permute-done.8 = bf16[256,4096]{1,0:T(8,128)(2,1)} collective-permute-done((bf16[256,4096]{1,0:T(8,128)(2,1)}, bf16[256,4096]{1,0:T(8,128)(2,1)}, u32[]{:S(2)}, u32[]{:S(2)}) %collective-permute-start.8) | collective-permute-done | bytes 2097184 | tf_op jit(solution)/shard_map/ppermute | solution.py:55
  291.9 4.7 %fusion.8 = bf16[1,256,4096]{2,1,0:T(8,128)(2,1)} fusion(bf16[576,4096]{1,0:T(8,128)(2,1)S(1)} %bitcast.26, bf16[256,4096]{1,0:T(8,128)(2,1)} %collective-permute-done.8, bf16[576,512]{1,0:T(8,128)(2,1)S(1)} %get-tuple-element.9), kind=kOutput, calls=%fused_computation.20 | convolution fusion | flops 1211105280 | bytes 9207808 | tf_op jit(solution)/shard_map/dot_general | solution.py:34
  296.7 17.7 %collective-permute-done.7 = bf16[256,4096]{1,0:T(8,128)(2,1)} collective-permute-done((bf16[256,4096]{1,0:T(8,128)(2,1)}, bf16[256,4096]{1,0:T(8,128)(2,1)}, u32[]{:S(2)}, u32[]{:S(2)}) %collective-permute-start.7) | collective-permute-done | bytes 2097184 | tf_op jit(solution)/shard_map/ppermute | solution.py:55
  314.4 4.7 %fusion.9 = bf16[1,256,4096]{2,1,0:T(8,128)(2,1)} fusion(bf16[576,4096]{1,0:T(8,128)(2,1)S(1)} %bitcast.26, bf16[256,4096]{1,0:T(8,128)(2,1)} %collective-permute-done.7, bf16[576,512]{1,0:T(8,128)(2,1)S(1)} %get-tuple-element.8), kind=kOutput, calls=%fused_computation.21 | convolution fusion | flops 1211105280 | bytes 9207808 | tf_op jit(solution)/shard_map/dot_general | solution.py:34
  319.1 3.6 %reshape.98 = bf16[288,4096]{1,0:T(8,128)(2,1)S(1)} reshape(bf16[32,288,128]{2,1,0:T(8,128)(2,1)} %all-to-all-done.3) | data formatting | bytes 4718592 | tf_op jit(solution)/shard_map/reshape | solution.py:26
  324.5 3.7 %reshape.99 = bf16[288,4096,1]{1,0,2:T(8,128)(2,1)S(1)} reshape(bf16[32,288,128]{2,1,0:T(8,128)(2,1)} %all-to-all-done.1) | data formatting | bytes 4718592 | tf_op jit(solution)/shard_map/reshape | solution.py:26
  328.2 4.5 %multiply_reduce_fusion = (f32[128,2]{0,1:T(2,128)}, bf16[128,4096]{1,0:T(8,128)(2,1)}) fusion(f32[128,4096]{1,0:T(8,128)} %convert_element_type.94, f32[128,2]{0,1:T(2,128)S(1)} %copy-done.7, bf16[288,4096,1]{1,0,2:T(8,128)(2,1)S(1)} %reshape.99, pred[128,2,288]{2,1,0:T(4,128)(4,1)} %eq.54), kind=kOutput, calls=%fused_computation.26 | convolution fusion | flops 607649536 | bytes 5580800 | tf_op jit(solution)/shard_map/dot_general | solution.py:34
  (78 shorter events, 41.1 us)
Async XLA Ops:
  0.6 2.2 copy-start
  3.6 11.2 %copy-start.5 = (bf16[128,4096]{1,0:T(8,128)(2,1)S(1)}, bf16[128,4096]{1,0:T(8,128)(2,1)}, u32[]{:S(2)}) copy-start(bf16[128,4096]{1,0:T(8,128)(2,1)} %param.13) | copy-start | bytes 3145732
  6.1 39.5 %all-to-all-start = ((bf16[32,288,128]{2,1,0:T(8,128)(2,1)}), bf16[32,288,128]{2,1,0:T(8,128)(2,1)}, u32[]{:S(2)}, u32[]{:S(2)}) async-start(bf16[32,288,128]{2,1,0:T(8,128)(2,1)} %reshape.91), calls=%async_computation | async-start | bytes 4718592 | tf_op jit(solution)/shard_map/all_to_all | solution.py:25
  18.9 6.2 %copy-start.7 = (f32[128,2]{0,1:T(2,128)S(1)}, f32[128,2]{0,1:T(2,128)}, u32[]{:S(2)}) copy-start(f32[128,2]{0,1:T(2,128)} %param.9) | copy-start | bytes 3076
  45.6 37.8 %all-to-all-start.2 = ((bf16[32,288,128]{2,1,0:T(8,128)(2,1)}), bf16[32,288,128]{2,1,0:T(8,128)(2,1)}, u32[]{:S(2)}, u32[]{:S(2)}) async-start(bf16[32,288,128]{2,1,0:T(8,128)(2,1)} %reshape.95), calls=%async_computation.2 | async-start | bytes 4718592 | tf_op jit(solution)/shard_map/all_to_all | solution.py:25
  56.2 37.9 %collective-permute-start = (bf16[288,4096]{1,0:T(8,128)(2,1)S(1)}, bf16[288,4096]{1,0:T(8,128)(2,1)}, u32[]{:S(2)}, u32[]{:S(2)}) collective-permute-start(bf16[288,4096]{1,0:T(8,128)(2,1)S(1)} %reshape.92), channel_id=1, source_target_pairs={{0,32},{1,97},{2,34},{3,99},{4,36},{5,101},{6,38},{7,103},{8,40},{... | collective-permute-start | bytes 7077896 | tf_op jit(solution)/shard_map/ppermute | solution.py:52
  88.4 5.6 %copy-start.4 = (bf16[288,4096]{1,0:T(8,128)(2,1)S(1)}, bf16[288,4096]{1,0:T(8,128)(2,1)}, u32[]{:S(2)}) copy-start(bf16[288,4096]{1,0:T(8,128)(2,1)} %reshape.96) | copy-start | bytes 7077892
  88.4 51.9 %collective-permute-start.5 = (bf16[288,4096]{1,0:T(8,128)(2,1)}, bf16[288,4096]{1,0:T(8,128)(2,1)S(1)}, u32[]{:S(2)}, u32[]{:S(2)}) collective-permute-start(bf16[288,4096]{1,0:T(8,128)(2,1)} %reshape.96), channel_id=1, source_target_pairs={{0,32},{1,97},{2,34},{3,99},{4,36},{5,101},{6,38},{7,103},{8,40},{... | collective-permute-start | bytes 7077896 | tf_op jit(solution)/shard_map/ppermute | solution.py:52
  92.1 48.4 %collective-permute-start.2 = (bf16[256,4096]{1,0:T(8,128)(2,1)}, bf16[256,4096]{1,0:T(8,128)(2,1)S(1)}, u32[]{:S(2)}, u32[]{:S(2)}) collective-permute-start(bf16[256,4096]{1,0:T(8,128)(2,1)} %bitcast.31), channel_id=1, source_target_pairs={{0,96},{1,33},{2,98},{3,35},{4,100},{5,37},{6,102},{7,39},{8,104},... | collective-permute-start | bytes 6291464 | tf_op jit(solution)/shard_map/ppermute | solution.py:55
  92.1 72.5 %collective-permute-start.3 = (bf16[256,4096]{1,0:T(8,128)(2,1)}, bf16[256,4096]{1,0:T(8,128)(2,1)S(1)}, u32[]{:S(2)}, u32[]{:S(2)}) collective-permute-start(bf16[256,4096]{1,0:T(8,128)(2,1)} %bitcast.35), channel_id=1, source_target_pairs={{0,96},{1,33},{2,98},{3,35},{4,100},{5,37},{6,102},{7,39},{8,104},... | collective-permute-start | bytes 6291464 | tf_op jit(solution)/shard_map/ppermute | solution.py:55
  93.6 93.2 %collective-permute-start.1 = (bf16[256,4096]{1,0:T(8,128)(2,1)}, bf16[256,4096]{1,0:T(8,128)(2,1)S(1)}, u32[]{:S(2)}, u32[]{:S(2)}) collective-permute-start(bf16[256,4096]{1,0:T(8,128)(2,1)} %bitcast.27), channel_id=1, source_target_pairs={{0,96},{1,33},{2,98},{3,35},{4,100},{5,37},{6,102},{7,39},{8,104},... | collective-permute-start | bytes 6291464 | tf_op jit(solution)/shard_map/ppermute | solution.py:55
  94.1 46.4 %copy-start.8 = (bf16[1,256,4096]{2,1,0:T(8,128)(2,1)S(1)}, bf16[1,256,4096]{2,1,0:T(8,128)(2,1)}, u32[]{:S(2)}) copy-start(bf16[1,256,4096]{2,1,0:T(8,128)(2,1)} %param.11) | copy-start | bytes 6291460
  96.2 90.6 %copy-start.2 = (bf16[576,4096]{1,0:T(8,128)(2,1)}, bf16[576,4096]{1,0:T(8,128)(2,1)S(1)}, u32[]{:S(2)}) copy-start(bf16[576,4096]{1,0:T(8,128)(2,1)S(1)} %constant_dynamic-update-slice_fusion) | copy-start | bytes 14155780
  140.5 24.1 %copy-start.3 = (bf16[576,4096]{1,0:T(8,128)(2,1)}, bf16[576,4096]{1,0:T(8,128)(2,1)S(1)}, u32[]{:S(2)}) copy-start(bf16[576,4096]{1,0:T(8,128)(2,1)S(1)} %constant_dynamic-update-slice_fusion.2) | copy-start | bytes 14155780
  140.5 24.1 %copy-start.9 = (bf16[1,256,4096]{2,1,0:T(8,128)(2,1)S(1)}, bf16[1,256,4096]{2,1,0:T(8,128)(2,1)}, u32[]{:S(2)}) copy-start(bf16[1,256,4096]{2,1,0:T(8,128)(2,1)} %param.12) | copy-start | bytes 6291460
  143.1 43.6 %copy-start.6 = (bf16[1,256,4096]{2,1,0:T(8,128)(2,1)S(1)}, bf16[1,256,4096]{2,1,0:T(8,128)(2,1)}, u32[]{:S(2)}) copy-start(bf16[1,256,4096]{2,1,0:T(8,128)(2,1)} %param.10) | copy-start | bytes 6291460
  164.6 29.5 %copy-start.11 = (bf16[256,4096]{1,0:T(8,128)(2,1)}, bf16[256,4096]{1,0:T(8,128)(2,1)S(1)}, u32[]{:S(2)}) copy-start(bf16[256,4096]{1,0:T(8,128)(2,1)S(1)} %collective-permute-done.3) | copy-start | bytes 6291460
  193.1 29.0 %collective-permute-start.6 = (bf16[288,4096]{1,0:T(8,128)(2,1)S(1)}, bf16[288,4096]{1,0:T(8,128)(2,1)S(1)}, u32[]{:S(2)}, u32[]{:S(2)}) collective-permute-start(bf16[288,4096]{1,0:T(8,128)(2,1)S(1)} %fusion.3), channel_id=1, source_target_pairs={{0,32},{1,97},{2,34},{3,99},{4,36},{5,101},{6,38},{7,103},{8,40},{... | collective-permute-start | bytes 7077896 | tf_op jit(solution)/shard_map/ppermute | solution.py:52
  197.0 52.9 %collective-permute-start.4 = (bf16[288,4096]{1,0:T(8,128)(2,1)}, bf16[288,4096]{1,0:T(8,128)(2,1)}, u32[]{:S(2)}, u32[]{:S(2)}) collective-permute-start(bf16[288,4096]{1,0:T(8,128)(2,1)} %convolution_convert_fusion.1), channel_id=1, source_target_pairs={{0,32},{1,97},{2,34},{3,99},{4,36},{5,101},{6,38},{7,103},{8,40},{... | collective-permute-start | bytes 7077896 | tf_op jit(solution)/shard_map/ppermute | solution.py:52
  229.8 10.8 %slice-start = ((s8[4718592]{0:T(1024)(128)(4,1)}), s8[524288]{0:T(1024)(128)(4,1)S(1)}, s32[]{:S(2)}) async-start(s8[4718592]{0:T(1024)(128)(4,1)} %bitcast.23), calls=%async_computation.4 | async-start | bytes 1048576
  229.8 35.9 %all-to-all-start.3 = ((bf16[32,288,128]{2,1,0:T(8,128)(2,1)}), bf16[32,288,128]{2,1,0:T(8,128)(2,1)}, u32[]{:S(2)}, u32[]{:S(2)}) async-start(bf16[32,288,128]{2,1,0:T(8,128)(2,1)} %reshape.97), calls=%async_computation.3 | async-start | bytes 4718592 | tf_op jit(solution)/shard_map/all_to_all | solution.py:25
  234.8 5.7 %slice-start.1 = ((s8[4718592]{0:T(1024)(128)(4,1)}), s8[4194304]{0:T(1024)(128)(4,1)S(1)}, s32[]{:S(2)}) async-start(s8[4718592]{0:T(1024)(128)(4,1)} %bitcast.23), calls=%async_computation.5 | async-start | bytes 8388608
  240.5 35.0 %collective-permute-start.9 = (bf16[256,4096]{1,0:T(8,128)(2,1)}, bf16[256,4096]{1,0:T(8,128)(2,1)}, u32[]{:S(2)}, u32[]{:S(2)}) collective-permute-start(bf16[256,4096]{1,0:T(8,128)(2,1)} %convolution_convert_fusion.3), channel_id=1, source_target_pairs={{0,96},{1,33},{2,98},{3,35},{4,100},{5,37},{6,102},{7,39},{8,104},... | collective-permute-start | bytes 6291464 | tf_op jit(solution)/shard_map/ppermute | solution.py:55
  243.7 6.2 %copy-start.10 = (bf16[1,256,4096]{2,1,0:T(8,128)(2,1)S(1)}, bf16[1,256,4096]{2,1,0:T(8,128)(2,1)}, u32[]{:S(2)}) copy-start(bf16[1,256,4096]{2,1,0:T(8,128)(2,1)} %param.12) | copy-start | bytes 6291460
  243.7 6.2 %copy-start.12 = (bf16[256,4096]{1,0:T(8,128)(2,1)S(1)}, bf16[256,4096]{1,0:T(8,128)(2,1)}, u32[]{:S(2)}) copy-start(bf16[256,4096]{1,0:T(8,128)(2,1)} %copy-done.11) | copy-start | bytes 6291460
  243.7 48.2 %collective-permute-start.8 = (bf16[256,4096]{1,0:T(8,128)(2,1)}, bf16[256,4096]{1,0:T(8,128)(2,1)}, u32[]{:S(2)}, u32[]{:S(2)}) collective-permute-start(bf16[256,4096]{1,0:T(8,128)(2,1)} %convolution_convert_fusion.4), channel_id=1, source_target_pairs={{0,96},{1,33},{2,98},{3,35},{4,100},{5,37},{6,102},{7,39},{8,104},... | collective-permute-start | bytes 6291464 | tf_op jit(solution)/shard_map/ppermute | solution.py:55
  248.3 66.1 %collective-permute-start.7 = (bf16[256,4096]{1,0:T(8,128)(2,1)}, bf16[256,4096]{1,0:T(8,128)(2,1)}, u32[]{:S(2)}, u32[]{:S(2)}) collective-permute-start(bf16[256,4096]{1,0:T(8,128)(2,1)} %convolution_convert_fusion.5), channel_id=1, source_target_pairs={{0,96},{1,33},{2,98},{3,35},{4,100},{5,37},{6,102},{7,39},{8,104},... | collective-permute-start | bytes 6291464 | tf_op jit(solution)/shard_map/ppermute | solution.py:55
  265.7 58.8 %all-to-all-start.1 = ((bf16[32,288,128]{2,1,0:T(8,128)(2,1)}), bf16[32,288,128]{2,1,0:T(8,128)(2,1)}, u32[]{:S(2)}, u32[]{:S(2)}) async-start(bf16[32,288,128]{2,1,0:T(8,128)(2,1)} %reshape.93), calls=%async_computation.1 | async-start | bytes 4718592 | tf_op jit(solution)/shard_map/all_to_all | solution.py:25
  274.7 17.2 %slice-start.2 = ((s8[4718592]{0:T(1024)(128)(4,1)}), s8[524288]{0:T(1024)(128)(4,1)S(1)}, s32[]{:S(2)}) async-start(s8[4718592]{0:T(1024)(128)(4,1)} %bitcast.25), calls=%async_computation.6 | async-start | bytes 1048576
  275.5 16.4 %slice-start.3 = ((s8[4718592]{0:T(1024)(128)(4,1)}), s8[4194304]{0:T(1024)(128)(4,1)S(1)}, s32[]{:S(2)}) async-start(s8[4718592]{0:T(1024)(128)(4,1)} %bitcast.25), calls=%async_computation.7 | async-start | bytes 8388608
  324.5 8.2 %copy-start.1 = (bf16[128,4096]{1,0:T(8,128)(2,1)S(1)}, bf16[128,4096]{1,0:T(8,128)(2,1)}, u32[]{:S(2)}) copy-start(bf16[128,4096]{1,0:T(8,128)(2,1)} %param.7) | copy-start | bytes 3145732
